TPU v7x, 32 devices: a whole 2x2x4 slice. The times are simulated.
32 devices in a mesh: fsdp: 8 (over z, y), tp: 4 (over x, core).
Axes of the slice: x: 2, y: 2, z: 4, core: 2. Of those that a mesh axis runs over, the one named last changes fastest.
Arguments:
- tokens: bfloat16 [2048, 4096], P('fsdp', 'tp'), may hold values from -6 to 6
- cotangent: bfloat16 [2048, 4096], P('fsdp', 'tp'), may hold values from -6 to 6
- up_weight: bfloat16 [4096, 14336], P('fsdp', 'tp'), may hold values from -0.1875 to 0.1875
- down_weight: bfloat16 [4096, 14336], P('fsdp', 'tp'), may hold values from -0.09375 to 0.09375
- up_list: int32 [4, 256, 2], P('tp'), may hold values from 0 to 31, as said below
- up_count: int32 [4], P('tp'), may hold values from 60 to 256, as said below
- down_list: int32 [4, 256, 2], P('tp'), may hold values from 0 to 31, as said below
- down_count: int32 [4], P('tp'), may hold values from 60 to 256, as said below
Outputs:
- mixed: bfloat16 [2048, 4096], P('fsdp', 'tp')
- grad_tokens: bfloat16 [2048, 4096], P('fsdp', 'tp')
- grad_up: float32 [4096, 14336], P('fsdp', 'tp')
- grad_down: float32 [4096, 14336], P('fsdp', 'tp')
Inputs may be any that keep to these rules, and one draw needn't show every extreme that they name: `up_list`: in each slice's list the first count entries are distinct pairs (row block below 32, column block below 28), in no particular order; every row block has at least one and at most 8 of them; in every slice all 4 row blocks held by some index of fsdp have exactly 8, and in some slice every row block has exactly 8. Entries from the count on are arbitrary pairs in range and carry no meaning. `up_count`: the number of valid entries of each slice's up list. `down_list`: as for up_list. `down_count`: the number of valid entries of each slice's down list.
All inputs are finite; a program needn't handle non-finite values.
Results may differ from a plain program's by a relative error of at most 0.015.
Values may be sent and summed in bfloat16 or wider, within the bound.
A program may use at most 256 MiB of HBM per device.

v0:
```python
import jax
import jax.numpy as jnp
from jax import lax
from jax.sharding import PartitionSpec as P

BLK = 128


SQRT_TWO_PI = 0.7978845608028654
CUBIC = 0.044715


def gelu_tanh(values):
    inner = SQRT_TWO_PI * (values + CUBIC * values * values * values)
    return 0.5 * values * (1.0 + jnp.tanh(inner))


def gelu_slope(values):
    tangent = jnp.tanh(SQRT_TWO_PI * (values + CUBIC * values * values * values))
    return 0.5 * (1.0 + tangent) + 0.5 * values * (1.0 - tangent * tangent) * SQRT_TWO_PI * (
        1.0 + 3.0 * CUBIC * values * values
    )


def list_table(entries, number):
    valid = jnp.arange(entries.shape[0], dtype=jnp.int32) < number
    return (entries[:, 0], entries[:, 1], valid)


def slot_table(entries, number, owner_blocks, owners, capacity):
    rows, cols, valid = list_table(entries, number)
    owner = rows // owner_blocks
    member = (
        (owner[:, None] == jnp.arange(owners, dtype=jnp.int32)[None, :]) & valid[:, None]
    ).astype(jnp.int32)
    earlier = jnp.cumsum(member, axis=0) - member
    rank = jnp.sum(earlier * member, axis=1)
    slot = owner * capacity + rank
    chosen = (
        valid[:, None] & (slot[:, None] == jnp.arange(owners * capacity, dtype=jnp.int32)[None, :])
    ).astype(jnp.int32)
    slot_rows = jnp.sum(chosen * rows[:, None], axis=0)
    slot_cols = jnp.sum(chosen * cols[:, None], axis=0)
    slot_valid = jnp.sum(chosen, axis=0) > 0
    return (slot_rows, slot_cols, slot_valid)


def pick_blocks(weight, table, row_offset):
    rows, cols, valid = table
    row_count = weight.shape[0] // BLK
    col_count = weight.shape[1] // BLK
    tiles = weight.reshape(row_count, BLK, col_count, BLK)
    local_rows = jnp.clip(rows - row_offset, 0, row_count - 1)
    picked = tiles[local_rows, :, cols, :]
    return jnp.where(valid[:, None, None], picked, jnp.zeros((), weight.dtype))


def place_grads(tiles, table, first_block, block_count, col_blocks):
    rows, cols, valid = table
    inside = valid & (rows >= first_block) & (rows < first_block + block_count)
    local_rows = jnp.clip(rows - first_block, 0, block_count - 1)
    kept = jnp.where(inside[:, None, None], tiles, jnp.zeros((), jnp.float32))
    spread = (
        jnp.zeros((block_count, BLK, col_blocks, BLK), jnp.float32)
        .at[local_rows, :, cols, :]
        .add(kept)
    )
    return spread.reshape(block_count * BLK, col_blocks * BLK)


def fetch(up_weight, down_weight, up_table, down_table, capacity, owner_blocks):
    first_slot = lax.axis_index("fsdp") * capacity
    up_mine = tuple((lax.dynamic_slice_in_dim(member, first_slot, capacity) for member in up_table))
    down_mine = tuple(
        (lax.dynamic_slice_in_dim(member, first_slot, capacity) for member in down_table)
    )
    offset = lax.axis_index("fsdp") * owner_blocks
    return (
        lax.all_gather(pick_blocks(up_weight, up_mine, offset), "fsdp", axis=0, tiled=True),
        lax.all_gather(pick_blocks(down_weight, down_mine, offset), "fsdp", axis=0, tiled=True),
    )


def body(tokens, cotangent, up_weight, down_weight, up_list, up_count, down_list, down_count):
    owner_blocks = up_weight.shape[0] // BLK
    col_blocks = up_weight.shape[1] // BLK
    owners = lax.axis_size("fsdp")
    group_rows = tokens.shape[0]
    up_table = slot_table(
        up_list[0],
        up_count[0],
        owner_blocks,
        owners,
        owner_blocks * (up_list.shape[1] // (owners * owner_blocks)),
    )
    down_table = slot_table(
        down_list[0],
        down_count[0],
        owner_blocks,
        owners,
        owner_blocks * (down_list.shape[1] // (owners * owner_blocks)),
    )
    capacity = up_list.shape[1] // owners
    up_blocks, down_blocks = fetch(
        up_weight, down_weight, up_table, down_table, capacity, owner_blocks
    )
    gathered = lax.all_gather(tokens, "tp", axis=1, tiled=True)
    width = gathered.shape[1]
    row_blocks = width // BLK
    x_tiles = gathered.reshape(group_rows, row_blocks, BLK)
    x_taken = jnp.take(x_tiles, up_table[0], axis=1)
    partial_up = jnp.einsum("rsk,skn->rsn", x_taken, up_blocks, preferred_element_type=jnp.float32)
    hidden = (
        jnp.zeros((group_rows, col_blocks, BLK), jnp.float32).at[:, up_table[1], :].add(partial_up)
    )
    active = gelu_tanh(hidden).astype(jnp.bfloat16)
    active_taken = jnp.take(active, down_table[1], axis=1)
    layer_product = jnp.einsum(
        "rsn,skn->rsk", active_taken, down_blocks, preferred_element_type=jnp.float32
    )
    layer_parts = (
        jnp.zeros((group_rows, row_blocks, BLK), jnp.float32)
        .at[:, down_table[0], :]
        .add(layer_product)
    )
    mixed = lax.psum_scatter(
        layer_parts.reshape(group_rows, width).astype(jnp.bfloat16),
        "tp",
        scatter_dimension=1,
        tiled=True,
    )
    up_again, down_again = fetch(
        up_weight, down_weight, up_table, down_table, capacity, owner_blocks
    )
    grad_in = lax.all_gather(cotangent, "tp", axis=1, tiled=True)
    dy_tiles = grad_in.reshape(group_rows, row_blocks, BLK)
    dy_taken = jnp.take(dy_tiles, down_table[0], axis=1)
    back_down = jnp.einsum("rsk,skn->rsn", dy_taken, down_again, preferred_element_type=jnp.float32)
    grad_active = (
        jnp.zeros((group_rows, col_blocks, BLK), jnp.float32).at[:, down_table[1], :].add(back_down)
    )
    grad_hidden = (grad_active * gelu_slope(hidden)).astype(jnp.bfloat16)
    hidden_taken = jnp.take(grad_hidden, up_table[1], axis=1)
    back_up = jnp.einsum("rsn,skn->rsk", hidden_taken, up_again, preferred_element_type=jnp.float32)
    input_parts = (
        jnp.zeros((group_rows, row_blocks, BLK), jnp.float32).at[:, up_table[0], :].add(back_up)
    )
    grad_tokens = lax.psum_scatter(
        input_parts.reshape(group_rows, width).astype(jnp.bfloat16),
        "tp",
        scatter_dimension=1,
        tiled=True,
    )
    up_rows_part = up_table[0]
    up_cols_part = up_table[1]
    down_rows_part = down_table[0]
    down_cols_part = down_table[1]
    x_part = jnp.take(x_tiles, up_rows_part, axis=1)
    hidden_part = jnp.take(grad_hidden, up_cols_part, axis=1)
    dy_part = jnp.take(dy_tiles, down_rows_part, axis=1)
    active_part = jnp.take(active, down_cols_part, axis=1)
    up_term = jnp.einsum("rsk,rsn->skn", x_part, hidden_part, preferred_element_type=jnp.float32)
    down_term = jnp.einsum("rsk,rsn->skn", dy_part, active_part, preferred_element_type=jnp.float32)
    summed = lax.psum_scatter(
        jnp.stack([up_term, down_term], axis=1).astype(jnp.bfloat16),
        "fsdp",
        scatter_dimension=0,
        tiled=True,
    ).astype(jnp.float32)
    first_slot = lax.axis_index("fsdp") * capacity
    offset = lax.axis_index("fsdp") * owner_blocks
    up_mine = tuple((lax.dynamic_slice_in_dim(member, first_slot, capacity) for member in up_table))
    down_mine = tuple(
        (lax.dynamic_slice_in_dim(member, first_slot, capacity) for member in down_table)
    )
    grad_up = place_grads(summed[:, 0], up_mine, offset, owner_blocks, col_blocks)
    grad_down = place_grads(summed[:, 1], down_mine, offset, owner_blocks, col_blocks)
    return (mixed, grad_tokens, grad_up, grad_down)


def solution(mesh):
    return jax.shard_map(
        body,
        mesh=mesh,
        in_specs=(
            P("fsdp", "tp"),
            P("fsdp", "tp"),
            P("fsdp", "tp"),
            P("fsdp", "tp"),
            P("tp", None, None),
            P("tp"),
            P("tp", None, None),
            P("tp"),
        ),
        out_specs=(P("fsdp", "tp"), P("fsdp", "tp"), P("fsdp", "tp"), P("fsdp", "tp")),
        check_vma=False,
    )
```

profile of v0, /device:TPU:0, one launch (start us, length us, event | category | flops | bytes accessed | tf_op | source)
XLA Modules:
  0.0 1044.7 jit_solution(11323882387440292511)
XLA Ops:
  16.0 7.1 reshape.260
  23.2 5.4 copy.67
  34.5 7.1 reshape.261
  41.6 5.5 copy.69
  60.2 4.1 copy.72
  64.3 9.6 gather_fusion.2
  73.9 11.2 %gather_fusion.4 = bf16[256,256,128]{2,1,0:T(8,128)(2,1)} fusion(bf16[256,32,128]{2,0,1:T(8,128)(2,1)} %copy.72, s32[1024]{0:T(1024)S(1)} %pad_clamp_fusion.1), kind=kCustom, calls=%fused_computation.2.clone | custom fusion | bytes 33555456 | tf_op jit(solution)/shard_map/jit(_take)/gather | solution.py:137
  85.1 102.2 %all-gather.7.cloned.1.call-done = bf16[256,128,128]{2,1,0:T(8,128)(2,1)} async-done(((bf16[32,128,128]{2,1,0:T(8,128)(2,1)}), bf16[256,128,128]{2,1,0:T(8,128)(2,1)}) %all-gather.7.cloned.1.call-update) | async-done | bytes 8388624 | tf_op jit(solution)/shard_map/all_gather | solution.py:79
  187.3 21.9 %fusion.12 = f32[256,256,128]{2,1,0:T(8,128)} fusion(bf16[256,128,128]{2,1,0:T(8,128)(2,1)} %all-gather.7.cloned.1.call-done, bf16[256,256,128]{2,1,0:T(8,128)(2,1)} %gather_fusion.2, pred[256]{0:T(512)(128)(4,1)S(1)} %get-tuple-element.51), kind=kOutput, calls=%fused_computation.26 | convolution fusion | flops 2155872256 | bytes 58720512 | tf_op jit(solution)/shard_map/rsk,skn->rsn/dot_general | solution.py:112
  211.5 73.8 %scatter_fusion = f32[256,28,128]{2,0,1:T(8,128)} fusion(f32[256,28,128]{2,0,1:T(8,128)} %broadcast.203.clone.1, s32[256]{0:T(256)S(1)} %bitcast.183, f32[256,256,128]{2,1,0:T(8,128)} %fusion.12), kind=kCustom, calls=%fused_computation.6 | custom fusion | flops 8388608 | bytes 100664320 | tf_op jit(solution)/shard_map/scatter-add | solution.py:114
  285.3 27.2 %all-gather.5.cloned.1.call-done = bf16[256,128,128]{2,1,0:T(8,128)(2,1)} async-done(((bf16[32,128,128]{2,1,0:T(8,128)(2,1)}), bf16[256,128,128]{2,1,0:T(8,128)(2,1)}) %all-gather.5.cloned.1.call-update) | async-done | bytes 8388624 | tf_op jit(solution)/shard_map/all_gather | solution.py:80
  312.5 21.8 %fusion.6 = f32[256,256,128]{2,1,0:T(8,128)} fusion(bf16[256,128,128]{2,1,0:T(8,128)(2,1)} %all-gather.5.cloned.1.call-done, bf16[256,256,128]{2,1,0:T(8,128)(2,1)} %gather_fusion.4, pred[256]{0:T(512)(128)(4,1)S(1)} %get-tuple-element.46), kind=kOutput, calls=%fused_computation.20 | convolution fusion | flops 2155872256 | bytes 58720512 | tf_op jit(solution)/shard_map/rsk,skn->rsn/dot_general | solution.py:138
  336.5 74.3 %scatter_fusion.2 = f32[256,28,128]{2,0,1:T(8,128)} fusion(f32[256,28,128]{2,0,1:T(8,128)} %broadcast.203.clone, s32[256]{0:T(256)S(1)} %bitcast.182, f32[256,256,128]{2,1,0:T(8,128)} %fusion.6), kind=kCustom, calls=%fused_computation.8 | custom fusion | flops 8388608 | bytes 100664320 | tf_op jit(solution)/shard_map/scatter-add | solution.py:140
  410.8 5.6 fusion.28
  416.4 11.1 %gather_fusion.5 = bf16[256,256,128]{2,1,0:T(8,128)(2,1)} fusion(bf16[256,28,128]{2,0,1:T(8,128)(2,1)} %get-tuple-element.34, s32[1024]{0:T(1024)S(1)} %pad_clamp_fusion), kind=kCustom, calls=%fused_computation.3.clone | custom fusion | bytes 33555456 | tf_op jit(solution)/shard_map/jit(_take)/gather | solution.py:143
  427.6 20.1 %fusion.2 = f32[256,256,128]{2,1,0:T(8,128)} fusion(bf16[256,128,128]{2,1,0:T(8,128)(2,1)} %all-gather.7.cloned.1.call-done, bf16[256,256,128]{2,1,0:T(8,128)(2,1)} %gather_fusion.5, pred[256]{0:T(512)(128)(4,1)S(1)} %get-tuple-element.50), kind=kOutput, calls=%fused_computation.16 | convolution fusion | flops 2155872256 | bytes 58720512 | tf_op jit(solution)/shard_map/rsn,skn->rsk/dot_general | solution.py:144
  450.2 71.0 %scatter_fusion.3 = f32[256,32,128]{2,0,1:T(8,128)} fusion(f32[256,32,128]{2,0,1:T(8,128)} %broadcast.195.clone.1, s32[256]{0:T(256)S(1)} %bitcast.181, f32[256,256,128]{2,1,0:T(8,128)} %fusion.2), kind=kCustom, calls=%fused_computation.9 | custom fusion | flops 8388608 | bytes 100664320 | tf_op jit(solution)/shard_map/scatter-add | solution.py:146
  525.0 4.1 copy.73
  529.2 9.6 gather_fusion.3
  538.8 20.2 %fusion.9 = f32[256,256,128]{2,1,0:T(8,128)} fusion(bf16[256,128,128]{2,1,0:T(8,128)(2,1)} %all-gather.5.cloned.1.call-done, bf16[256,256,128]{2,1,0:T(8,128)(2,1)} %gather_fusion.3, pred[256]{0:T(512)(128)(4,1)S(1)} %copy-done.10), kind=kOutput, calls=%fused_computation.23 | convolution fusion | flops 2155872256 | bytes 58720512 | tf_op jit(solution)/shard_map/rsn,skn->rsk/dot_general | solution.py:118
  561.5 71.4 %scatter_fusion.1 = f32[256,32,128]{2,0,1:T(8,128)} fusion(f32[256,32,128]{2,0,1:T(8,128)} %broadcast.195.clone, s32[256]{0:T(256)S(1)} %bitcast.184, f32[256,256,128]{2,1,0:T(8,128)} %fusion.9), kind=kCustom, calls=%fused_computation.7 | custom fusion | flops 8388608 | bytes 100664320 | tf_op jit(solution)/shard_map/scatter-add | solution.py:124
  638.4 16.9 %convert_bitcast_fusion = bf16[256,1,128,128]{3,2,0,1:T(8,128)(2,1)} fusion(bf16[256,256,128]{2,1,0:T(8,128)(2,1)} %gather_fusion.3, pred[256]{0:T(512)(128)(4,1)S(1)} %copy-done.10, bf16[256,256,128]{2,1,0:T(8,128)(2,1)} %gather_fusion.4, pred[256]{0:T(512)(128)(4,1)S(1)} %copy-done.9), kind=kOutput, calls=%fused_computation.32 | convolution fusion | flops 2168455168 | bytes 41943552 | tf_op jit(solution)/shard_map/rsk,rsn->skn/dot_general | solution.py:163
  655.4 17.2 %convert_bitcast_fusion.1 = bf16[256,1,128,128]{3,2,0,1:T(8,128)(2,1)} fusion(bf16[256,256,128]{2,1,0:T(8,128)(2,1)} %gather_fusion.2, pred[256]{0:T(512)(128)(4,1)S(1)} %copy-done.7, bf16[256,256,128]{2,1,0:T(8,128)(2,1)} %gather_fusion.5, pred[256]{0:T(512)(128)(4,1)S(1)} %get-tuple-element.50), kind=kOutput, calls=%fused_computation.33 | convolution fusion | flops 2168455168 | bytes 41943552 | tf_op jit(solution)/shard_map/rsk,rsn->skn/dot_general | solution.py:162
  672.6 8.0 pad_maximum_fusion
  682.6 12.2 %copy.102 = bf16[32,8,256,128]{3,1,2,0:T(8,128)(2,1)} copy(bf16[32,8,256,128]{3,2,1,0:T(8,128)(2,1)S(1)} %bitcast.162) | data formatting | bytes 33554432
  698.9 276.6 %reduce-scatter.11.cloned.1.call-done = bf16[32,32768]{1,0:T(8,128)(2,1)} async-done(((bf16[256,32768]{1,0:T(8,128)(2,1)}), bf16[32,32768]{1,0:T(8,128)(2,1)}) %reduce-scatter.11.cloned.1.call-update) | async-done | bytes 2097168
  983.8 7.7 scatter_fusion.5
  991.4 7.4 copy.89
  998.8 10.1 copy.103
  1012.9 7.0 scatter_fusion.4
  1019.9 7.4 copy.88
  1027.3 10.1 copy.104
  (109 shorter events, 63.6 us)
Async XLA Ops:
  7.2 46.1 %all-gather.9.cloned.1.call-start = ((), (), s32[]{:S(2)}) async-start(), calls=%async_computation.5 | async-start | bytes 2621440 | tf_op jit(solution)/shard_map/all_gather | solution.py:107
  9.3 50.9 %all-gather.11.cloned.1.call-start = ((), (), s32[]{:S(2)}) async-start(), calls=%async_computation.7 | async-start | bytes 2621440 | tf_op jit(solution)/shard_map/all_gather | solution.py:135
  11.4 175.9 %all-gather.7.cloned.1.call-start = ((), (), s32[]{:S(2)}) async-start(), calls=%async_computation.4 | async-start | bytes 9437184 | tf_op jit(solution)/shard_map/all_gather | solution.py:79
  29.3 23.5 %copy-start.2 = (s32[256]{0:T(256)}, s32[256]{0:T(256)S(1)}, u32[]{:S(2)}) copy-start(s32[256]{0:T(256)S(1)} %get-tuple-element.27) | copy-start | bytes 3076
  29.3 23.5 %copy-start.4 = (s32[256]{0:T(256)}, s32[256]{0:T(256)S(1)}, u32[]{:S(2)}) copy-start(s32[256]{0:T(256)S(1)} %get-tuple-element.26) | copy-start | bytes 3076
  34.5 278.0 %all-gather.5.cloned.1.call-start = ((), (), s32[]{:S(2)}) async-start(), calls=%async_computation.3 | async-start | bytes 9437184 | tf_op jit(solution)/shard_map/all_gather | solution.py:80
  51.8 643.0 %reduce-scatter.9.cloned.1.call-start = ((), (), s32[]{:S(2)}) async-start(), calls=%async_computation.8 | async-start | bytes 2621440 | tf_op jit(solution)/shard_map/reduce_scatter | solution.py:148
  52.7 134.6 %copy-start.6 = (pred[256]{0:T(512)(128)(4,1)}, pred[256]{0:T(512)(128)(4,1)S(1)}, u32[]{:S(2)}) copy-start(pred[256]{0:T(512)(128)(4,1)S(1)} %get-tuple-element.51) | copy-start | bytes 772
  53.3 259.2 %copy-start.8 = (pred[256]{0:T(512)(128)(4,1)}, pred[256]{0:T(512)(128)(4,1)S(1)}, u32[]{:S(2)}) copy-start(pred[256]{0:T(512)(128)(4,1)S(1)} %get-tuple-element.46) | copy-start | bytes 772
  427.6 22.6 %copy-start.11 = (s32[256,1]{0,1:T(1,128)S(1)}, s32[256,1]{0,1:T(1,128)}, u32[]{:S(2)}) copy-start(s32[256,1]{0,1:T(1,128)} %compare_select_fusion.1) | copy-start | bytes 3076
  521.2 8.0 copy-start.5
  521.2 8.0 copy-start.3
  529.1 167.8 %reduce-scatter.7.cloned.1.call-start = ((), (), s32[]{:S(2)}) async-start(), calls=%async_computation.6 | async-start | bytes 2621440 | tf_op jit(solution)/shard_map/reduce_scatter | solution.py:126
  529.2 9.6 copy-start.10
  632.9 5.5 copy-start.9
  638.3 17.0 %copy-start.7 = (pred[256]{0:T(512)(128)(4,1)S(1)}, pred[256]{0:T(512)(128)(4,1)}, u32[]{:S(2)}) copy-start(pred[256]{0:T(512)(128)(4,1)} %copy-done.6) | copy-start | bytes 772
  638.4 337.1 %reduce-scatter.11.cloned.1.call-start = ((), (), s32[]{:S(2)}) async-start(), calls=%async_computation.9 | async-start | bytes 18874368
  694.8 283.3 %copy-start.12 = (pred[32]{0:T(512)(128)(4,1)S(1)}, pred[32]{0:T(512)(128)(4,1)}, u32[]{:S(2)}) copy-start(pred[32]{0:T(512)(128)(4,1)} %get-tuple-element.30) | copy-start | bytes 100
  694.8 283.3 %copy-start.13 = (pred[32]{0:T(512)(128)(4,1)S(1)}, pred[32]{0:T(512)(128)(4,1)}, u32[]{:S(2)}) copy-start(pred[32]{0:T(512)(128)(4,1)} %get-tuple-element.28) | copy-start | bytes 100
  978.1 5.7 copy-start.1
  998.8 14.1 %copy-start = (s32[32]{0:T(128)S(1)}, s32[32]{0:T(128)}, u32[]{:S(2)}) copy-start(s32[32]{0:T(128)} %get-tuple-element.38) | copy-start | bytes 388
Sparse Core Ops, SparseCore 0:
  10.1 25.2 all-gather.8
  37.6 22.5 all-gather.10
  62.3 124.9 all-gather.6
  189.3 123.1 all-gather.4
  529.2 29.3 reduce-scatter.8
  638.5 28.9 reduce-scatter.6
  694.9 280.5 reduce-scatter.10
where the time goes:
time: 1050 us; the launch traced here: 1040 us
  waiting for transfers between devices  410 us (39%)
  other arithmetic  336 us (32%)
  local copies, waits for them, and re-layouts  164 us (16%)
  matrix products  118 us (11%)
  between operations  16.3 us (2%)
    unnamed x8, waiting for transfers between devices  277 us
    all_gather x1, waiting for transfers between devices, fetch(): lax.all_gather(pick_blocks(up_weight, up_mine, offset), 'fsdp', axis=0, t...  102 us
    scatter-add x1, other arithmetic, body(): jnp.zeros((group_rows, col_blocks, BLK), jnp.float32)  74.3 us
    scatter-add x1, other arithmetic, body(): jnp.zeros((group_rows, col_blocks, BLK), jnp.float32).at[:, up_table[1], :]  73.8 us
    scatter-add x1, other arithmetic, body(): layer_parts = jnp.zeros((group_rows, row_blocks, BLK), jnp.float32).at[:,...  71.4 us
    scatter-add x1, other arithmetic, body(): jnp.zeros((group_rows, row_blocks, BLK), jnp.float32).at[:, up_table[0], :]  71 us
    unnamed x39, local copies, waits for them, and re-layouts  59.5 us
    all_gather x1, waiting for transfers between devices, fetch(): lax.all_gather(pick_blocks(down_weight, down_mine, offset), 'fsdp', axis=...  27.2 us
  transfers between devices with their start and end apart: 7, of which 4 were waited for; matrix products, arithmetic and copies ran while one was open for 32% of the time, Pallas kernels for 0%

commit v1 on v0

v1 whole, which is shorter than its diff:
```python
import functools

import jax
import jax.numpy as jnp
from jax import lax
from jax.experimental import pallas as pl
from jax.experimental.pallas import tpu as pltpu
from jax.sharding import PartitionSpec as P

BLK = 128
SQRT_TWO_PI = 0.7978845608028654
CUBIC = 0.044715
F32 = jnp.float32
BF16 = jnp.bfloat16


def tables(entries, counts, row_blocks, col_blocks, cap):
    length = entries.shape[1]
    rows, cols = entries[:, :, 0], entries[:, :, 1]
    at = jnp.arange(length, dtype=jnp.int32)
    valid = at[None, :] < counts[:, None]
    earlier = (rows[:, :, None] == rows[:, None, :]) & (at[None, None, :] < at[None, :, None])
    rank = jnp.sum((earlier & valid[:, None, :]).astype(jnp.int32), axis=2)
    slot = jnp.where(valid, rows * cap + rank, -1)
    slots = jnp.arange(row_blocks * cap, dtype=jnp.int32)
    chosen = slot[:, None, :] == slots[None, :, None]
    slot_cols = jnp.sum(jnp.where(chosen, cols[:, None, :] + 1, 0), axis=2) - 1
    place = jnp.where(valid, rows * col_blocks + cols, -1)
    places = jnp.arange(row_blocks * col_blocks, dtype=jnp.int32)
    here = place[:, None, :] == places[None, :, None]
    rank_of = jnp.sum(jnp.where(here, rank[:, None, :] - cap, 0), axis=2) + cap
    return slot_cols, rank_of.reshape(entries.shape[0], row_blocks, col_blocks)


def pick_kernel(cap, cols_ref, up_ref, down_ref, out_ref, sems):
    count = out_ref.shape[0] // 2
    for side, weight in enumerate((up_ref, down_ref)):
        for s in range(count):
            col = pl.multiple_of(jnp.maximum(cols_ref[side, s], 0) * BLK, BLK)
            pltpu.make_async_copy(
                weight.at[pl.ds((s // cap) * BLK, BLK), pl.ds(col, BLK)],
                out_ref.at[side * count + s],
                sems.at[side * count + s],
            ).start()
    for side, weight in enumerate((up_ref, down_ref)):
        for s in range(count):
            pltpu.make_async_copy(
                weight.at[pl.ds((s // cap) * BLK, BLK), pl.ds(0, BLK)],
                out_ref.at[side * count + s],
                sems.at[side * count + s],
            ).wait()

            @pl.when(cols_ref[side, s] < 0)
            def _():
                out_ref[side * count + s] = jnp.zeros((BLK, BLK), BF16)


def pick(cols, up_weight, down_weight, cap):
    count = cols.shape[1]
    return pl.pallas_call(
        functools.partial(pick_kernel, cap),
        out_shape=jax.ShapeDtypeStruct((2 * count, BLK, BLK), BF16),
        in_specs=[
            pl.BlockSpec(memory_space=pltpu.SMEM),
            pl.BlockSpec(memory_space=pl.ANY),
            pl.BlockSpec(memory_space=pl.ANY),
        ],
        out_specs=pl.BlockSpec(memory_space=pltpu.VMEM),
        scratch_shapes=[pltpu.SemaphoreType.DMA((2 * count,))],
        name="pick_blocks",
    )(cols, up_weight, down_weight)


def place_kernel(cap, cols_ref, sum_ref, up_ref, down_ref):
    row = pl.program_id(0)
    for side, out in enumerate((up_ref, down_ref)):
        out[...] = jnp.zeros_like(out)
        for j in range(cap):
            col = cols_ref[side, row * cap + j]

            @pl.when(col >= 0)
            def _():
                out[:, pl.ds(pl.multiple_of(col * BLK, BLK), BLK)] = sum_ref[side, j].astype(F32)


def place(cols, summed, cap, col_blocks):
    count = cols.shape[1]
    spec = pl.BlockSpec((BLK, col_blocks * BLK), lambda r: (r, 0))
    shape = jax.ShapeDtypeStruct((count // cap * BLK, col_blocks * BLK), F32)
    return pl.pallas_call(
        functools.partial(place_kernel, cap),
        grid=(count // cap,),
        out_shape=(shape, shape),
        in_specs=[
            pl.BlockSpec(memory_space=pltpu.SMEM),
            pl.BlockSpec((2, cap, BLK, BLK), lambda r: (0, r, 0, 0)),
        ],
        out_specs=(spec, spec),
        compiler_params=pltpu.CompilerParams(vmem_limit_bytes=32 << 20),
        name="place_grads",
    )(cols, summed)


MESH = pl.DeviceIdType.MESH
PIECES = 4


def dot_t(left, right):
    return lax.dot_general(left, right, (((1,), (1,)), ((), ())), preferred_element_type=F32)


def fused_kernel(
    n, ways, per, cap, cols, rank, picked, tokens, cotangent,
    mixed, grad_tokens, summed,
    x, dy, wu, wd, stage, hid, grad, act, gh, lay, inp, lay_in, inp_in, first, passing,
    local_sems, tp_send, tp_recv, ag_send, ag_recv, rs_send, rs_recv, back_send, back_recv,
):
    me_f = lax.axis_index("fsdp")
    me_t = lax.axis_index("tp")
    mine = per * cap
    npc = mine // PIECES
    half = max(1, per // 2)
    rowwise = per % PIECES == 0
    pairs = hid.shape[0]
    rows = n * per
    rpt = rows // ways
    width = rpt * BLK

    def at_position(q):
        q = lax.rem(q + 2 * n, n)
        high = q // (n // 2)
        return 2 * q * (1 - high) + (2 * n - 1 - 2 * q) * high

    odd = lax.rem(me_f, 2)
    here = (me_f // 2) * (1 - odd) + (n - 1 - me_f // 2) * odd
    target = (at_position(here + 1), at_position(here - 1))

    barrier = pltpu.get_barrier_semaphore()
    for f in target:
        pl.semaphore_signal(barrier, inc=1, device_id=(f, me_t), device_id_type=MESH)
    for i in range(1, ways):
        pl.semaphore_signal(
            barrier, inc=1, device_id=(me_f, lax.rem(me_t + i, ways)), device_id_type=MESH
        )

    weights = (wu, wd)
    spot = pl.ds(me_f * mine, mine)
    locals_ = [
        pltpu.make_async_copy(picked.at[pl.ds(0, mine)], wu.at[spot], local_sems.at[0]),
        pltpu.make_async_copy(picked.at[pl.ds(mine, mine)], wd.at[spot], local_sems.at[1]),
        pltpu.make_async_copy(tokens, x.at[me_t], local_sems.at[2]),
        pltpu.make_async_copy(cotangent, dy.at[me_t], local_sems.at[3]),
    ]
    for copy in locals_:
        copy.start()
    for copy in locals_:
        copy.wait()
    pl.semaphore_wait(barrier, 2 + ways - 1)

    def features(side, i):
        full = (x, dy)[side]
        return pltpu.make_async_remote_copy(
            src_ref=full.at[me_t],
            dst_ref=full.at[me_t],
            send_sem=tp_send.at[side, i],
            recv_sem=tp_recv.at[side, i],
            device_id=(me_f, lax.rem(me_t + i, ways)),
            device_id_type=MESH,
        )

    def hop(side, step, k, d):
        owner = at_position(here - step if d == 0 else here + step)
        block = weights[side].at[pl.ds(owner * mine + k * npc, npc)]
        return pltpu.make_async_remote_copy(
            src_ref=block,
            dst_ref=block,
            send_sem=ag_send.at[side, step, k],
            recv_sem=ag_recv.at[side, step, k],
            device_id=(target[d], me_t),
            device_id_type=MESH,
        )

    def arrived(side, step, k, d):
        owner = at_position(here - step - 1 if d == 0 else here + step + 1)
        block = weights[side].at[pl.ds(owner * mine + k * npc, npc)]
        return pltpu.make_async_remote_copy(
            src_ref=block,
            dst_ref=block,
            send_sem=ag_send.at[side, step, k],
            recv_sem=ag_recv.at[side, step, k],
            device_id=(target[d], me_t),
            device_id_type=MESH,
        )

    order = [(d * (PIECES // 2) + j, d) for j in range(PIECES // 2) for d in range(2)]

    def gather_start(side):
        for k, d in order:
            hop(side, 0, k, d).start()

    def gather_step(side, step, forward):
        for k, d in order:
            arrived(side, step, k, d).wait_recv()
            if forward:
                hop(side, step + 1, k, d).start()

    def spread(side, row, count):
        total = (hid, grad)[side]
        for i in range(count):
            stage[i, pl.ds(0, cap)] = weights[side][pl.ds((row + i) * cap, cap)]
        full = (x, dy)[side]
        part = full[row // rpt, :, pl.ds(pl.multiple_of(lax.rem(row, rpt) * BLK, BLK), count * BLK)]

        def column(c, carry):
            block = jnp.concatenate(
                [
                    jnp.concatenate(
                        [stage[i, rank[side, row + i, 2 * c + q]] for q in range(2)], axis=1
                    )
                    for i in range(count)
                ],
                axis=0,
            )
            total[c] += jnp.dot(part, block, preferred_element_type=F32)
            return carry

        lax.fori_loop(0, pairs, column, 0)

    def spread_arrived(side, step):
        if rowwise:
            for d in range(2):
                owner = at_position(here - step - 1 if d == 0 else here + step + 1)
                spread(side, owner * per + d * half, half)

    def spread_own(side):
        if rowwise:
            for d in range(2):
                spread(side, me_f * per + d * half, half)

    def spread_all(side):
        if not rowwise:

            def one(r, carry):
                spread(side, r, 1)
                return carry

            lax.fori_loop(0, rows, one, 0)

    def activate(c):
        v = hid[c]
        s = jnp.tanh(SQRT_TWO_PI * (v + CUBIC * v * v * v))
        a = (0.5 * v * (1.0 + s)).astype(BF16)
        act[2 * c] = a[:, :BLK]
        act[2 * c + 1] = a[:, BLK:]
        hid[c] = 0.5 * (1.0 + s) + 0.5 * v * (1.0 - s * s) * SQRT_TWO_PI * (1.0 + 3.0 * CUBIC * v * v)

    def finish(c, carry):
        g = (grad[c] * hid[c]).astype(BF16)
        gh[2 * c] = g[:, :BLK]
        gh[2 * c + 1] = g[:, BLK:]
        return carry

    def taken(side, start, count):
        values = (gh, act)[side]
        return jnp.concatenate([values[cols[side, start + j]] for j in range(count)], axis=1)

    def back(r):
        at = pl.ds(pl.multiple_of(lax.rem(r, rpt) * BLK, BLK), BLK)
        for side, out in ((0, inp), (1, lay)):
            block = jnp.concatenate([weights[side][r * cap + j] for j in range(cap)], axis=1)
            out[r // rpt, :, at] = dot_t(taken(side, r * cap, cap), block).astype(BF16)

    def term(side, owner, k):
        row = owner * per + (k * npc) // cap
        at = pl.ds(pl.multiple_of(lax.rem(row, rpt) * BLK, BLK), BLK)
        left = (x, dy)[side][row // rpt, :, at].T
        return jnp.dot(left, taken(side, owner * mine + k * npc, npc), preferred_element_type=F32)

    def send_sum(side, step, k, d, source):
        return pltpu.make_async_remote_copy(
            src_ref=source,
            dst_ref=passing.at[side, step, k],
            send_sem=rs_send.at[side, step, k],
            recv_sem=rs_recv.at[side, step, k],
            device_id=(target[d], me_t),
            device_id_type=MESH,
        )

    def scatter_start(side):
        for k, d in order:
            value = term(side, at_position(here - 1 if d == 0 else here + 1), k).astype(BF16)
            for j in range(npc):
                first[side, k, j] = value[:, j * BLK : (j + 1) * BLK]
            send_sum(side, 0, k, d, first.at[side, k]).start()

    def scatter_step(side, step):
        for k, d in order:
            value = term(side, at_position(here - step - 2 if d == 0 else here + step + 2), k)
            send_sum(side, step, k, d, passing.at[side, step, k]).wait_recv()
            for j in range(npc):
                passing[side, step, k, j] = (
                    passing[side, step, k, j].astype(F32) + value[:, j * BLK : (j + 1) * BLK]
                ).astype(BF16)
            send_sum(side, step + 1, k, d, passing.at[side, step, k]).start()

    def scatter_last(side):
        for k, d in order:
            value = term(side, me_f, k)
            send_sum(side, n - 2, k, d, passing.at[side, n - 2, k]).wait_recv()
            for j in range(npc):
                summed[side, k * npc + j] = (
                    passing[side, n - 2, k, j].astype(F32) + value[:, j * BLK : (j + 1) * BLK]
                )

    def share(side, i):
        out, into = ((inp, inp_in), (lay, lay_in))[side]
        to = lax.rem(me_t + i, ways)
        return pltpu.make_async_remote_copy(
            src_ref=out.at[to],
            dst_ref=into.at[i - 1],
            send_sem=back_send.at[side, i],
            recv_sem=back_recv.at[side, i],
            device_id=(me_f, to),
            device_id_type=MESH,
        )

    for i in range(1, ways):
        features(0, i).start()
    gather_start(0)
    hid[...] = jnp.zeros_like(hid)
    grad[...] = jnp.zeros_like(grad)
    for i in range(stage.shape[0]):
        stage[i, cap] = jnp.zeros((BLK, BLK), BF16)
    gather_step(0, 0, True)
    gather_step(0, 1, True)
    for i in range(1, ways):
        features(1, i).start()
    for i in range(1, ways):
        features(0, i).wait_recv()
    spread_own(0)

    def up_step(s, carry):
        gather_step(0, s, True)
        spread_arrived(0, s - 2)
        return carry

    lax.fori_loop(2, n - 2, up_step, 0)
    gather_start(1)
    spread_arrived(0, n - 4)
    gather_step(0, n - 2, False)
    spread_arrived(0, n - 3)
    spread_arrived(0, n - 2)
    spread_all(0)
    for i in range(1, ways):
        features(1, i).wait_recv()

    share_act = -(-pairs // (n - 2))

    def down_step(s, carry):
        gather_step(1, s, True)
        for i in range(share_act):

            @pl.when(s * share_act + i < pairs)
            def _():
                activate(s * share_act + i)

        spread_arrived(1, s)
        return carry

    lax.fori_loop(0, n - 2, down_step, 0)
    scatter_start(1)
    spread_own(1)
    gather_step(1, n - 2, False)
    spread_arrived(1, n - 2)
    spread_all(1)
    lax.fori_loop(0, pairs, finish, 0)

    share_rows = -(-rows // (n - 2))

    def down_sum(s, carry):
        scatter_step(1, s)

        def one(r, inner):
            back(r)
            return inner

        lax.fori_loop(s * share_rows, jnp.minimum((s + 1) * share_rows, rows), one, 0)
        return carry

    lax.fori_loop(0, n - 2, down_sum, 0)
    scatter_start(0)
    for side in range(2):
        for i in range(1, ways):
            share(side, i).start()
    scatter_last(1)

    def up_sum(s, carry):
        scatter_step(0, s)
        return carry

    lax.fori_loop(0, n - 2, up_sum, 0)
    for side, out, own, into in ((0, grad_tokens, inp, inp_in), (1, mixed, lay, lay_in)):
        for i in range(1, ways):
            share(side, i).wait_recv()
        total = own[me_t].astype(F32)
        for i in range(1, ways):
            total += into[i - 1].astype(F32)
        out[...] = total.astype(BF16)
    scatter_last(0)

    for side in range(2):
        for i in range(1, ways):
            features(side, i).wait_send()
            share(side, i).wait_send()

        def sent(s, carry):
            for k, d in order:
                hop(side, s, k, d).wait_send()
                send_sum(side, s, k, d, passing.at[side, s, k]).wait_send()
            return carry

        lax.fori_loop(0, n - 1, sent, 0)


def fused(cols, rank, picked, tokens, cotangent, n, ways, per, cap, col_blocks):
    group, width = tokens.shape
    rows = n * per
    npc = per * cap // PIECES
    half = max(1, per // 2)
    vmem = pl.BlockSpec(memory_space=pltpu.VMEM)
    smem = pl.BlockSpec(memory_space=pltpu.SMEM)
    hbm = pl.BlockSpec(memory_space=pl.ANY)
    dma = pltpu.SemaphoreType.DMA
    return pl.pallas_call(
        functools.partial(fused_kernel, n, ways, per, cap),
        out_shape=(
            jax.ShapeDtypeStruct((group, width), BF16),
            jax.ShapeDtypeStruct((group, width), BF16),
            jax.ShapeDtypeStruct((2, per * cap, BLK, BLK), F32),
        ),
        in_specs=[smem, smem, hbm, hbm, hbm],
        out_specs=(vmem, vmem, vmem),
        scratch_shapes=[
            pltpu.VMEM((ways, group, width), BF16),
            pltpu.VMEM((ways, group, width), BF16),
            pltpu.VMEM((rows * cap, BLK, BLK), BF16),
            pltpu.VMEM((rows * cap, BLK, BLK), BF16),
            pltpu.VMEM((half, cap + 1, BLK, BLK), BF16),
            pltpu.VMEM((col_blocks // 2, group, 2 * BLK), F32),
            pltpu.VMEM((col_blocks // 2, group, 2 * BLK), F32),
            pltpu.VMEM((col_blocks, group, BLK), BF16),
            pltpu.VMEM((col_blocks, group, BLK), BF16),
            pltpu.VMEM((ways, group, width), BF16),
            pltpu.VMEM((ways, group, width), BF16),
            pltpu.VMEM((ways - 1, group, width), BF16),
            pltpu.VMEM((ways - 1, group, width), BF16),
            pltpu.VMEM((2, PIECES, npc, BLK, BLK), BF16),
            pltpu.VMEM((2, n - 1, PIECES, npc, BLK, BLK), BF16),
            dma((4,)),
            dma((2, ways)),
            dma((2, ways)),
            dma((2, n - 1, PIECES)),
            dma((2, n - 1, PIECES)),
            dma((2, n - 1, PIECES)),
            dma((2, n - 1, PIECES)),
            dma((2, ways)),
            dma((2, ways)),
        ],
        compiler_params=pltpu.CompilerParams(
            collective_id=0, has_side_effects=True, vmem_limit_bytes=63 << 20
        ),
        name="fused_layer",
    )(cols, rank, picked, tokens, cotangent)


def body(tokens, cotangent, up_weight, down_weight, up_list, up_count, down_list, down_count):
    per = up_weight.shape[0] // BLK
    col_blocks = up_weight.shape[1] // BLK
    owners = lax.axis_size("fsdp")
    rows = per * owners
    cap = up_list.shape[1] // rows
    mine = per * cap
    entries = jnp.stack([up_list[0], down_list[0]])
    counts = jnp.stack([up_count[0], down_count[0]])
    cols, rank = tables(entries, counts, rows, col_blocks, cap)
    my_cols = lax.dynamic_slice_in_dim(cols, lax.axis_index("fsdp") * mine, mine, axis=1)
    picked = pick(my_cols, up_weight, down_weight, cap)
    mixed, grad_tokens, summed = fused(
        jnp.maximum(cols, 0), rank, picked, tokens, cotangent,
        owners, lax.axis_size("tp"), per, cap, col_blocks,
    )
    grad_up, grad_down = place(my_cols, summed, cap, col_blocks)
    return (mixed, grad_tokens, grad_up, grad_down)


def solution(mesh):
    return jax.shard_map(
        body,
        mesh=mesh,
        in_specs=(
            P("fsdp", "tp"),
            P("fsdp", "tp"),
            P("fsdp", "tp"),
            P("fsdp", "tp"),
            P("tp", None, None),
            P("tp"),
            P("tp", None, None),
            P("tp"),
        ),
        out_specs=(P("fsdp", "tp"), P("fsdp", "tp"), P("fsdp", "tp"), P("fsdp", "tp")),
        check_vma=False,
    )
```

time: 1050 us -> 350 us (0.33)
  waiting for transfers between devices: 410 us -> 0 us
  Pallas kernels: 0 us -> 339 us
  other arithmetic: 336 us -> 1.66 us
  local copies, waits for them, and re-layouts: 164 us -> 6.5 us
  matrix products: 118 us -> 0 us
  between operations: 16.3 us -> 1.98 us
    pallas_call x0 -> x3, Pallas kernels: none -> 339 us  [the longest x1 328 us: fused(): pl.pallas_call(functools.partial(fused_kernel, n, ways, per, cap), out_sh...]
    scatter-add x6 -> x0, other arithmetic: 305 us -> none  [the longest x1 74.3 us: body(): jnp.zeros((group_rows, col_blocks, BLK), jnp.float32)]
    unnamed x8 -> x0, waiting for transfers between devices: 277 us -> none
    all_gather x4 -> x0, waiting for transfers between devices: 133 us -> none  [the longest x1 102 us: fetch(): lax.all_gather(pick_blocks(up_weight, up_mine, offset), 'fsdp', axis=0, t...]
    dot_general x6 -> x0, matrix products: 118 us -> none  [the longest x1 21.9 us: body(): jnp.einsum('rsk,skn->rsn', x_taken, up_blocks, preferred_element_type=jnp...]
    unnamed x39 -> x12, local copies, waits for them, and re-layouts: 59.5 us -> 5.15 us
    gather x6 -> x0, local copies, waits for them, and re-layouts: 47.1 us -> none  [the longest x1 11.2 us: body(): dy_taken = jnp.take(dy_tiles, down_table[0], axis=1)]
    reshape x6 -> x0, local copies, waits for them, and re-layouts: 32.4 us -> none  [the longest x4 25.1 us: pick_blocks(): tiles = weight.reshape(row_count, BLK, col_count, BLK)]
  transfers between devices with their start and end apart: 7 -> 0, of which waited for: 4 -> 0; matrix products, arithmetic and copies ran while one was open for 32% -> 0% of each run, Pallas kernels for 0% -> 0%
where the time goes in v1:
time: 350 us; the launch traced here: 349 us
  Pallas kernels  339 us (97%)
  local copies, waits for them, and re-layouts  6.5 us (2%)
    pallas_call x1, Pallas kernels, fused(): pl.pallas_call(functools.partial(fused_kernel, n, ways, per, cap), out_sh...  328 us

profile of v1, /device:TPU:0, one launch (start us, length us, event | category | flops | bytes accessed | tf_op | source)
XLA Modules:
  0.0 349.1 jit_solution(1155357280934496843)
XLA Ops:
  1.9 0.1 pad_add_fusion.1
  2.0 0.1 iota_compare_fusion.3
  2.1 0.7 copy.16
  2.8 0.7 copy.17
  3.4 0.1 add_select_fusion
  3.5 0.3 convert_reduce_fusion
  3.8 0.1 broadcast_add_fusion.1
  3.9 0.2 select_reduce_fusion.1
  4.0 0.6 broadcast_add_fusion.3
  4.6 0.6 constant_dynamic-slice_fusion.cols_ref
  5.3 0.3 select_reduce_fusion
  5.6 0.7 add.51.rank
  6.3 4.4 %pick_blocks.1.picked = bf16[64,128,128]{2,1,0:T(8,128)(2,1)} custom-call(s32[2,32]{1,0:T(2,128)} %constant_dynamic-slice_fusion.cols_ref, bf16[512,3584]{1,0:T(8,128)(2,1)} %up_ref.1, bf16[512,3584]{1,0:T(8,128)(2,1)} %down_ref.1), custom_call_target="tpu_custom_call" | custom-call | tf_op jit(solution)/shard_map/pick_blocks/pallas_call | solution.py:60
  10.7 0.0 copy-start.1
  10.7 328.2 %fused_layer.1 = (bf16[256,1024]{1,0:T(8,128)(2,1)}, bf16[256,1024]{1,0:T(8,128)(2,1)}, f32[2,32,128,128]{3,2,1,0:T(8,128)}) custom-call(s32[2,256]{1,0:T(2,128)} %get-tuple-element.18.cols, s32[2,32,28]{2,1,0:T(8,128)} %add.51.rank, bf16[64,128,128]{2,1,0:T(8,128)(2,1)} %pick_blocks.1.picked, bf16[256,1024]{1,0:T(8,128)(2,1)} %tokens.1, ...), custom_call_target="tpu_custom_call" | custom-call | tf_op jit(solution)/shard_map/fused_layer/pallas_call | solution.py:434
  339.0 0.0 copy-done.1
  339.0 0.0 copy-start
  339.0 2.2 copy-done
  341.2 0.0 copy-start.3
  341.2 0.0 copy-start.2
  341.2 6.3 %place_grads.1 = (f32[512,3584]{1,0:T(8,128)}, f32[512,3584]{1,0:T(8,128)}) custom-call(s32[2,32]{1,0:T(2,128)S(1)} %copy-done.1, f32[2,32,128,128]{3,2,1,0:T(8,128)S(1)} %copy-done), custom_call_target="tpu_custom_call" | custom-call | tf_op jit(solution)/shard_map/place_grads/pallas_call | solution.py:90
  347.5 0.0 copy-done.3
  347.5 0.8 copy.22
  348.3 0.0 copy-done.2
  348.3 0.8 copy.23
  (2 shorter events, 0.0 us)
Async XLA Ops:
  10.7 328.3 %copy-start.1 = (s32[2,32]{1,0:T(2,128)S(1)}, s32[2,32]{1,0:T(2,128)}, u32[]{:S(2)}) copy-start(s32[2,32]{1,0:T(2,128)} %constant_dynamic-slice_fusion.cols_ref) | copy-start | bytes 772
  339.0 2.2 copy-start
  341.2 6.3 %copy-start.3 = (bf16[256,1024]{1,0:T(8,128)(2,1)S(1)}, bf16[256,1024]{1,0:T(8,128)(2,1)}, u32[]{:S(2)}) copy-start(bf16[256,1024]{1,0:T(8,128)(2,1)} %get-tuple-element.25) | copy-start | bytes 1572868
  341.2 7.1 %copy-start.2 = (bf16[256,1024]{1,0:T(8,128)(2,1)S(1)}, bf16[256,1024]{1,0:T(8,128)(2,1)}, u32[]{:S(2)}) copy-start(bf16[256,1024]{1,0:T(8,128)(2,1)} %get-tuple-element.26) | copy-start | bytes 1572868

commit v2 on v1

--- a/solution.py
+++ b/solution.py
@@ -71,8 +71,10 @@
     )(cols, up_weight, down_weight)
 
 
-def place_kernel(cap, cols_ref, sum_ref, up_ref, down_ref):
+def place_kernel(cap, cols_ref, sum_ref, mixed_in, grad_in, up_ref, down_ref, mixed_out, grad_out):
     row = pl.program_id(0)
+    mixed_out[...] = mixed_in[...]
+    grad_out[...] = grad_in[...]
     for side, out in enumerate((up_ref, down_ref)):
         out[...] = jnp.zeros_like(out)
         for j in range(cap):
@@ -80,25 +82,32 @@
 
             @pl.when(col >= 0)
             def _():
-                out[:, pl.ds(pl.multiple_of(col * BLK, BLK), BLK)] = sum_ref[side, j].astype(F32)
-
-
-def place(cols, summed, cap, col_blocks):
+                out[:, pl.ds(pl.multiple_of(col * BLK, BLK), BLK)] = sum_ref[side, j]
+
+
+def place(cols, summed, mixed, grad_tokens, cap, col_blocks):
     count = cols.shape[1]
-    spec = pl.BlockSpec((BLK, col_blocks * BLK), lambda r: (r, 0))
-    shape = jax.ShapeDtypeStruct((count // cap * BLK, col_blocks * BLK), F32)
+    per, cuts = count // cap, 2
+    group, width = mixed.shape
+    depth = BLK // cuts
+    spec = pl.BlockSpec((depth, col_blocks * BLK), lambda r, h: (r * cuts + h, 0))
+    shape = jax.ShapeDtypeStruct((per * BLK, col_blocks * BLK), F32)
+    through = pl.BlockSpec((group // (per * cuts), width), lambda r, h: (r * cuts + h, 0))
+    same = jax.ShapeDtypeStruct(mixed.shape, BF16)
     return pl.pallas_call(
         functools.partial(place_kernel, cap),
-        grid=(count // cap,),
-        out_shape=(shape, shape),
+        grid=(per, cuts),
+        out_shape=(shape, shape, same, same),
         in_specs=[
             pl.BlockSpec(memory_space=pltpu.SMEM),
-            pl.BlockSpec((2, cap, BLK, BLK), lambda r: (0, r, 0, 0)),
+            pl.BlockSpec((2, cap, depth, BLK), lambda r, h: (0, r, h, 0)),
+            through,
+            through,
         ],
-        out_specs=(spec, spec),
-        compiler_params=pltpu.CompilerParams(vmem_limit_bytes=32 << 20),
+        out_specs=(spec, spec, through, through),
+        compiler_params=pltpu.CompilerParams(vmem_limit_bytes=60 << 20),
         name="place_grads",
-    )(cols, summed)
+    )(cols, summed, mixed, grad_tokens)
 
 
 MESH = pl.DeviceIdType.MESH
@@ -112,8 +121,8 @@
 def fused_kernel(
     n, ways, per, cap, cols, rank, picked, tokens, cotangent,
     mixed, grad_tokens, summed,
-    x, dy, wu, wd, stage, hid, grad, act, gh, lay, inp, lay_in, inp_in, first, passing,
-    local_sems, tp_send, tp_recv, ag_send, ag_recv, rs_send, rs_recv, back_send, back_recv,
+    final, x, dy, wu, wd, stage, hid, grad, act, gh, lay, inp, lay_in, inp_in, first, passing,
+    local_sems, out_sems, tp_send, tp_recv, ag_send, ag_recv, rs_send, rs_recv, back_send, back_recv,
 ):
     me_f = lax.axis_index("fsdp")
     me_t = lax.axis_index("tp")
@@ -153,8 +162,8 @@
     ]
     for copy in locals_:
         copy.start()
-    for copy in locals_:
-        copy.wait()
+    locals_[0].wait()
+    locals_[2].wait()
     pl.semaphore_wait(barrier, 2 + ways - 1)
 
     def features(side, i):
@@ -192,17 +201,17 @@
             device_id_type=MESH,
         )
 
-    order = [(d * (PIECES // 2) + j, d) for j in range(PIECES // 2) for d in range(2)]
-
-    def gather_start(side):
-        for k, d in order:
+    order = [(k, k // (PIECES // 2)) for k in range(PIECES)]
+    streams = [[(d * (PIECES // 2) + j, d) for d in range(2)] for j in range(PIECES // 2)]
+
+    def gather_start(side, j):
+        for k, d in streams[j]:
             hop(side, 0, k, d).start()
 
-    def gather_step(side, step, forward):
-        for k, d in order:
+    def gather_step(side, step, j):
+        for k, d in streams[j]:
             arrived(side, step, k, d).wait_recv()
-            if forward:
-                hop(side, step + 1, k, d).start()
+            hop(side, step + 1, k, d).start()
 
     def spread(side, row, count):
         total = (hid, grad)[side]
@@ -226,16 +235,14 @@
 
         lax.fori_loop(0, pairs, column, 0)
 
-    def spread_arrived(side, step):
+    def spread_arrived(side, step, d):
         if rowwise:
-            for d in range(2):
-                owner = at_position(here - step - 1 if d == 0 else here + step + 1)
-                spread(side, owner * per + d * half, half)
-
-    def spread_own(side):
+            owner = at_position(here - step - 1 if d == 0 else here + step + 1)
+            spread(side, owner * per + d * half, half)
+
+    def spread_own(side, d):
         if rowwise:
-            for d in range(2):
-                spread(side, me_f * per + d * half, half)
+            spread(side, me_f * per + d * half, half)
 
     def spread_all(side):
         if not rowwise:
@@ -264,11 +271,16 @@
         values = (gh, act)[side]
         return jnp.concatenate([values[cols[side, start + j]] for j in range(count)], axis=1)
 
-    def back(r):
-        at = pl.ds(pl.multiple_of(lax.rem(r, rpt) * BLK, BLK), BLK)
-        for side, out in ((0, inp), (1, lay)):
+    def back(side, start, stop):
+        out = (inp, lay)[side]
+
+        def one(r, carry):
+            at = pl.ds(pl.multiple_of(lax.rem(r, rpt) * BLK, BLK), BLK)
             block = jnp.concatenate([weights[side][r * cap + j] for j in range(cap)], axis=1)
             out[r // rpt, :, at] = dot_t(taken(side, r * cap, cap), block).astype(BF16)
+            return carry
+
+        lax.fori_loop(jnp.minimum(start, rows), jnp.minimum(stop, rows), one, 0)
 
     def term(side, owner, k):
         row = owner * per + (k * npc) // cap
@@ -286,31 +298,43 @@
             device_id_type=MESH,
         )
 
-    def scatter_start(side):
-        for k, d in order:
+    def first_terms(side, j):
+        for k, d in streams[j]:
             value = term(side, at_position(here - 1 if d == 0 else here + 1), k).astype(BF16)
-            for j in range(npc):
-                first[side, k, j] = value[:, j * BLK : (j + 1) * BLK]
-            send_sum(side, 0, k, d, first.at[side, k]).start()
-
-    def scatter_step(side, step):
-        for k, d in order:
-            value = term(side, at_position(here - step - 2 if d == 0 else here + step + 2), k)
+            for i in range(npc):
+                first[side, k, i] = value[:, i * BLK : (i + 1) * BLK]
+
+    def scatter_start(side, k, d):
+        send_sum(side, 0, k, d, first.at[side, k]).start()
+
+    def scatter_step(side, step, j):
+        values = [
+            term(side, at_position(here - step - 2 if d == 0 else here + step + 2), k)
+            for k, d in streams[j]
+        ]
+        for value, (k, d) in zip(values, streams[j]):
             send_sum(side, step, k, d, passing.at[side, step, k]).wait_recv()
-            for j in range(npc):
-                passing[side, step, k, j] = (
-                    passing[side, step, k, j].astype(F32) + value[:, j * BLK : (j + 1) * BLK]
+            for i in range(npc):
+                passing[side, step, k, i] = (
+                    passing[side, step, k, i].astype(F32) + value[:, i * BLK : (i + 1) * BLK]
                 ).astype(BF16)
             send_sum(side, step + 1, k, d, passing.at[side, step, k]).start()
 
-    def scatter_last(side):
-        for k, d in order:
-            value = term(side, me_f, k)
+    def result(side, k):
+        spot = pl.ds(k * npc, npc)
+        return pltpu.make_async_copy(final.at[side, spot], summed.at[side, spot], out_sems.at[side, k])
+
+    def scatter_last(side, j, after):
+        values = [term(side, me_f, k) for k, d in streams[j]]
+        for k, d in streams[j]:
             send_sum(side, n - 2, k, d, passing.at[side, n - 2, k]).wait_recv()
-            for j in range(npc):
-                summed[side, k * npc + j] = (
-                    passing[side, n - 2, k, j].astype(F32) + value[:, j * BLK : (j + 1) * BLK]
+            after(k, d)
+        for value, (k, d) in zip(values, streams[j]):
+            for i in range(npc):
+                final[side, k * npc + i] = (
+                    passing[side, n - 2, k, i].astype(F32) + value[:, i * BLK : (i + 1) * BLK]
                 )
+            result(side, k).start()
 
     def share(side, i):
         out, into = ((inp, inp_in), (lay, lay_in))[side]
@@ -324,89 +348,124 @@
             device_id_type=MESH,
         )
 
+    gather_start(0, 0)
     for i in range(1, ways):
         features(0, i).start()
-    gather_start(0)
     hid[...] = jnp.zeros_like(hid)
     grad[...] = jnp.zeros_like(grad)
     for i in range(stage.shape[0]):
         stage[i, cap] = jnp.zeros((BLK, BLK), BF16)
-    gather_step(0, 0, True)
-    gather_step(0, 1, True)
+    gather_start(0, 1)
+    locals_[1].wait()
+    locals_[3].wait()
+    for step in range(2):
+        gather_step(0, step, 0)
+        gather_step(0, step, 1)
     for i in range(1, ways):
         features(1, i).start()
     for i in range(1, ways):
         features(0, i).wait_recv()
-    spread_own(0)
+    for d in range(2):
+        spread_own(0, d)
 
     def up_step(s, carry):
-        gather_step(0, s, True)
-        spread_arrived(0, s - 2)
+        for j in range(2):
+            gather_step(0, s, j)
+            spread_arrived(0, s - 2, j)
         return carry
 
     lax.fori_loop(2, n - 2, up_step, 0)
-    gather_start(1)
-    spread_arrived(0, n - 4)
-    gather_step(0, n - 2, False)
-    spread_arrived(0, n - 3)
-    spread_arrived(0, n - 2)
+    for j in range(2):
+        for k, d in streams[j]:
+            arrived(0, n - 2, k, d).wait_recv()
+            hop(1, 0, k, d).start()
+        spread_arrived(0, n - 4, j)
+        spread_arrived(0, n - 3, j)
+
+    share_act = -(-pairs // (2 * (n - 3)))
+    for d in range(2):
+        spread_arrived(0, n - 2, d)
     spread_all(0)
     for i in range(1, ways):
         features(1, i).wait_recv()
-
-    share_act = -(-pairs // (n - 2))
+    for j in range(2):
+        gather_step(1, 0, j)
+        spread_own(1, j)
 
     def down_step(s, carry):
-        gather_step(1, s, True)
-        for i in range(share_act):
-
-            @pl.when(s * share_act + i < pairs)
-            def _():
-                activate(s * share_act + i)
-
-        spread_arrived(1, s)
+        for j in range(2):
+            gather_step(1, s, j)
+            for i in range(share_act):
+                c = ((s - 1) * 2 + j) * share_act + i
+
+                @pl.when(c < pairs)
+                def _():
+                    activate(c)
+
+            spread_arrived(1, s - 1, j)
         return carry
 
-    lax.fori_loop(0, n - 2, down_step, 0)
-    scatter_start(1)
-    spread_own(1)
-    gather_step(1, n - 2, False)
-    spread_arrived(1, n - 2)
+    lax.fori_loop(1, n - 2, down_step, 0)
+    for j in range(2):
+        first_terms(1, j)
+        for k, d in streams[j]:
+            arrived(1, n - 2, k, d).wait_recv()
+            scatter_start(1, k, d)
+        spread_arrived(1, n - 3, j)
+    for d in range(2):
+        spread_arrived(1, n - 2, d)
     spread_all(1)
-    lax.fori_loop(0, pairs, finish, 0)
-
-    share_rows = -(-rows // (n - 2))
+
+    middle = pairs // 2
+    scatter_step(1, 0, 0)
+    lax.fori_loop(0, middle, finish, 0)
+    scatter_step(1, 0, 1)
+    lax.fori_loop(middle, pairs, finish, 0)
+    lay_rows = -(-rows // (2 * (n - 3)))
 
     def down_sum(s, carry):
-        scatter_step(1, s)
-
-        def one(r, inner):
-            back(r)
-            return inner
-
-        lax.fori_loop(s * share_rows, jnp.minimum((s + 1) * share_rows, rows), one, 0)
+        for j in range(2):
+            scatter_step(1, s, j)
+            back(1, ((s - 1) * 2 + j) * lay_rows, ((s - 1) * 2 + j + 1) * lay_rows)
         return carry
 
-    lax.fori_loop(0, n - 2, down_sum, 0)
-    scatter_start(0)
-    for side in range(2):
-        for i in range(1, ways):
-            share(side, i).start()
-    scatter_last(1)
+    lax.fori_loop(1, n - 2, down_sum, 0)
+    for i in range(1, ways):
+        share(1, i).start()
+    for j in range(2):
+        first_terms(0, j)
+        scatter_last(1, j, lambda k, d: scatter_start(0, k, d))
+
+    early = max(1, n - 4)
+    inp_rows = -(-rows // (2 * early))
 
     def up_sum(s, carry):
-        scatter_step(0, s)
+        for j in range(2):
+            scatter_step(0, s, j)
+            back(0, (s * 2 + j) * inp_rows, (s * 2 + j + 1) * inp_rows)
         return carry
 
-    lax.fori_loop(0, n - 2, up_sum, 0)
-    for side, out, own, into in ((0, grad_tokens, inp, inp_in), (1, mixed, lay, lay_in)):
+    def up_sum_late(s, carry):
+        for j in range(2):
+            scatter_step(0, s, j)
+        return carry
+
+    def collect(side, out, own, into):
         for i in range(1, ways):
             share(side, i).wait_recv()
         total = own[me_t].astype(F32)
         for i in range(1, ways):
             total += into[i - 1].astype(F32)
         out[...] = total.astype(BF16)
-    scatter_last(0)
+
+    lax.fori_loop(0, early, up_sum, 0)
+    for i in range(1, ways):
+        share(0, i).start()
+    collect(1, mixed, lay, lay_in)
+    lax.fori_loop(early, n - 2, up_sum_late, 0)
+    scatter_last(0, 0, lambda k, d: None)
+    collect(0, grad_tokens, inp, inp_in)
+    scatter_last(0, 1, lambda k, d: None)
 
     for side in range(2):
         for i in range(1, ways):
@@ -420,6 +479,8 @@
             return carry
 
         lax.fori_loop(0, n - 1, sent, 0)
+        for k in range(PIECES):
+            result(side, k).wait()
 
 
 def fused(cols, rank, picked, tokens, cotangent, n, ways, per, cap, col_blocks):
@@ -439,8 +500,9 @@
             jax.ShapeDtypeStruct((2, per * cap, BLK, BLK), F32),
         ),
         in_specs=[smem, smem, hbm, hbm, hbm],
-        out_specs=(vmem, vmem, vmem),
+        out_specs=(vmem, vmem, hbm),
         scratch_shapes=[
+            pltpu.VMEM((2, per * cap, BLK, BLK), F32),
             pltpu.VMEM((ways, group, width), BF16),
             pltpu.VMEM((ways, group, width), BF16),
             pltpu.VMEM((rows * cap, BLK, BLK), BF16),
@@ -457,6 +519,7 @@
             pltpu.VMEM((2, PIECES, npc, BLK, BLK), BF16),
             pltpu.VMEM((2, n - 1, PIECES, npc, BLK, BLK), BF16),
             dma((4,)),
+            dma((2, PIECES)),
             dma((2, ways)),
             dma((2, ways)),
             dma((2, n - 1, PIECES)),
@@ -489,7 +552,9 @@
         jnp.maximum(cols, 0), rank, picked, tokens, cotangent,
         owners, lax.axis_size("tp"), per, cap, col_blocks,
     )
-    grad_up, grad_down = place(my_cols, summed, cap, col_blocks)
+    grad_up, grad_down, mixed, grad_tokens = place(
+        my_cols, summed, mixed, grad_tokens, cap, col_blocks
+    )
     return (mixed, grad_tokens, grad_up, grad_down)
 
 

time: 350 us -> 348 us (level)
  local copies, waits for them, and re-layouts: 6.5 us -> 2.73 us
    unnamed x12 -> x2, local copies, waits for them, and re-layouts: 5.15 us -> 1.37 us
where the time goes in v2:
time: 348 us
  Pallas kernels  342 us (98%)
    pallas_call x1, Pallas kernels, fused(): pl.pallas_call(functools.partial(fused_kernel, n, ways, per, cap), out_sh...  328 us
    pallas_call x1, Pallas kernels, place(): pl.pallas_call(functools.partial(place_kernel, cap), grid=(per, cuts), ou...  9.28 us

profile of v2, /device:TPU:0, one launch (start us, length us, event | category | flops | bytes accessed | tf_op | source)
XLA Modules:
  0.0 348.0 jit_solution(9704877517367018874)
XLA Ops:
  1.9 0.1 pad_add_fusion.1
  2.0 0.1 iota_compare_fusion.3
  2.1 0.7 copy.16
  2.8 0.7 copy.17
  3.4 0.1 add_select_fusion
  3.5 0.3 convert_reduce_fusion
  3.8 0.1 broadcast_add_fusion.1
  3.9 0.2 select_reduce_fusion.1
  4.0 0.6 broadcast_maximum_fusion
  4.6 0.6 constant_dynamic-slice_fusion.cols_ref
  5.3 0.3 select_reduce_fusion
  5.6 0.7 add.52.rank
  6.3 4.1 %pick_blocks.1.picked = bf16[64,128,128]{2,1,0:T(8,128)(2,1)} custom-call(s32[2,32]{1,0:T(2,128)} %constant_dynamic-slice_fusion.cols_ref, bf16[512,3584]{1,0:T(8,128)(2,1)} %up_ref.1, bf16[512,3584]{1,0:T(8,128)(2,1)} %down_ref.1), custom_call_target="tpu_custom_call" | custom-call | tf_op jit(solution)/shard_map/pick_blocks/pallas_call | solution.py:60
  10.5 328.2 %fused_layer.1 = (bf16[256,1024]{1,0:T(8,128)(2,1)}, bf16[256,1024]{1,0:T(8,128)(2,1)}, f32[2,32,128,128]{3,2,1,0:T(8,128)}) custom-call(s32[2,256]{1,0:T(2,128)} %get-tuple-element.23.cols, s32[2,32,28]{2,1,0:T(8,128)} %add.52.rank, bf16[64,128,128]{2,1,0:T(8,128)(2,1)} %pick_blocks.1.picked, bf16[256,1024]{1,0:T(8,128)(2,1)} %tokens.1, ...), custom_call_target="tpu_custom_call" | custom-call | tf_op jit(solution)/shard_map/fused_layer/pallas_call | solution.py:495
  338.7 9.3 %place_grads.1 = (f32[512,3584]{1,0:T(8,128)}, f32[512,3584]{1,0:T(8,128)}, bf16[256,1024]{1,0:T(8,128)(2,1)}, bf16[256,1024]{1,0:T(8,128)(2,1)}) custom-call(s32[2,32]{1,0:T(2,128)} %constant_dynamic-slice_fusion.cols_ref, f32[2,32,128,128]{3,2,1,0:T(8,128)} %get-tuple-element.11.sum_ref, bf16[256,1024]{1,0:T(8,128)(2,1)} %get-tuple-element.12.mixed_in, ...), custom_call_target="tpu_custom_call" | custom-call | tf_op jit(solution)/shard_map/place_grads/pallas_call | solution.py:97
  (2 shorter events, 0.0 us)
